TPU v7x, 128 devices: a whole 4x4x4 slice. The times are simulated.
128 devices in a mesh: run: 8 (over y, x_lo), mz: 16 (over z, x_hi, core).
Axes of the slice: x: 4 (x_hi: 2, x_lo: 2; x = x_hi * 2 + x_lo), y: 4, z: 4, core: 2. Of those that a mesh axis runs over, the one named last changes fastest.
Arguments:
- spectra: bfloat16 [98304, 4096], P('run', 'mz'), may hold values from -6 to 6
- mz_factor: bfloat16 [4096, 128], P('mz'), may hold values from -0.1125 to 0.1125
- mixing: float32 [128, 128], replicated, may hold values from -1 to 2, as said below
- run_weights: float32 [96, 128], P('run'), may hold values from 0.5 to 6
- block_count: int32 [8, 12], P('run'), may hold values from 1 to 8, 48 in all within a row
- trim_scans: int32 [8, 12], P('run'), may hold values from 0 to 56
Outputs:
- new_mz: float32 [4096, 128], P('mz')
- new_weights: float32 [96, 128], P('run')
Inputs may be any that keep to these rules, and one draw needn't show every extreme that they name: `mixing`: about the identity plus a dense part.
All inputs are finite; a program needn't handle non-finite values.
Results may differ from a plain program's by a relative error of at most 0.00071.
Values may be sent and summed in bfloat16 or wider, within the bound.
A program may use at most 128 MiB of HBM per device.

v0:
```python
import jax
import jax.numpy as jnp
from jax import lax
from jax.sharding import PartitionSpec as P

R = 128
BLOCK = 256
NSTEPS = 8
RUN_DEV = 12
SLOTS = 48


highest = lax.Precision.HIGHEST


def run_layout(counts, trims):
    starts = jnp.cumsum(counts) - counts
    block_ids = jnp.arange(SLOTS, dtype=jnp.int32)
    member = (block_ids[None, :] >= starts[:, None]) & (
        block_ids[None, :] < (starts + counts)[:, None]
    )
    final_block = block_ids[None, :] == (starts + counts - 1)[:, None]
    scan_limit = BLOCK - jnp.sum(jnp.where(final_block, trims[:, None], 0), axis=0)
    return (member.astype(jnp.float32), scan_limit)


def solve_right(matrix, values):
    lower = jnp.linalg.cholesky(matrix)
    return jax.scipy.linalg.cho_solve((lower, True), values.T).T


def shape_target(partial_value, live_rows, block_weights, mixing):
    scaled = partial_value * live_rows[:, :, None] * block_weights[:, None, :]
    return jnp.einsum("bir,sr->bis", scaled, mixing, precision=highest)


def run_gram(member, values):
    block_grams = jnp.einsum("bir,bis->brs", values, values, precision=highest)
    return jnp.einsum("kb,brs->krs", member, block_grams, precision=highest)


def apply_factors(member, values, factors):
    spread = jnp.einsum("kb,krs->brs", member, factors, precision=highest)
    return jnp.einsum("bir,brs->bis", values, spread, precision=highest)


def per_device(spectra, mz_factor, mixing, run_weights, block_count, trim_scans):
    mz_width = spectra.shape[1]
    member, scan_limit = run_layout(block_count[0], trim_scans[0])
    live_rows = (jnp.arange(BLOCK, dtype=jnp.int32)[None, :] < scan_limit[:, None]).astype(
        jnp.float32
    )
    block_weights = jnp.dot(member.T, run_weights, precision=highest)
    partial_value = jnp.dot(spectra, mz_factor, preferred_element_type=jnp.float32)
    scores = lax.psum(partial_value, "mz")
    target = shape_target(scores.reshape(SLOTS, BLOCK, R), live_rows, block_weights, mixing)
    square_sums = jnp.dot(member, jnp.sum(target * target, axis=(1, 2)), precision=highest)
    run_norm = jnp.sqrt(square_sums + 1e-06)
    iterate = target / jnp.dot(member.T, run_norm, precision=highest)[:, None, None]
    identity = jnp.eye(R, dtype=jnp.float32)
    for sweep in range(NSTEPS):
        coefficient = 1.5 * identity[None] - 0.5 * run_gram(member, iterate)
        iterate = apply_factors(member, iterate, coefficient)
    polar_rows = iterate.astype(jnp.bfloat16)
    spectra_blocks = spectra.reshape(SLOTS, BLOCK, mz_width)

    def accumulate(running, turn_index):
        first_row = turn_index * 8
        polar_block = lax.dynamic_slice_in_dim(polar_rows, first_row, 8, 0)
        spectra_block = lax.dynamic_slice_in_dim(spectra_blocks, first_row, 8, 0)
        member_block = lax.dynamic_slice_in_dim(member, first_row, 8, 1)
        products = jnp.einsum(
            "bir,bij->brj", polar_block, spectra_block, preferred_element_type=jnp.float32
        )
        return (
            running + jnp.einsum("kb,brj->krj", member_block, products, precision=highest),
            None,
        )

    projected, unused = lax.scan(
        accumulate,
        jnp.zeros((RUN_DEV, R, mz_width), jnp.float32),
        jnp.arange(SLOTS // 8, dtype=jnp.int32),
    )
    mix_gram = jnp.dot(mixing.T, mixing, precision=highest)
    scaled_mix = mixing[None, :, :] * run_weights[:, None, :]
    own_gram = jnp.dot(run_weights.T, run_weights, precision=highest)
    partial_terms = jnp.einsum("kij,kir->jr", projected, scaled_mix, precision=highest)
    gathered, weight_gram = lax.psum((partial_terms, own_gram), "run")
    new_mz = solve_right(weight_gram * mix_gram, gathered)
    along_mz = jnp.einsum("kij,jr->kir", projected, new_mz, precision=highest)
    equation_part = jnp.sum(along_mz * mixing[None, :, :], axis=1)
    mz_part = jnp.dot(new_mz.T, new_mz, precision=highest)
    equation, mz_gram = lax.psum((equation_part, mz_part), "mz")
    new_weights = solve_right(mz_gram * mix_gram, equation)
    return (new_mz, new_weights)


def solution(mesh):
    placed = (P("run", "mz"), P("mz", None), P(), P("run", None), P("run", None), P("run", None))
    return jax.shard_map(
        per_device,
        mesh=mesh,
        in_specs=placed,
        out_specs=(P("mz", None), P("run", None)),
        check_vma=False,
    )
```

profile of v0, /device:TPU:1, one launch (start us, length us, event | category | flops | bytes accessed | tf_op | source)
XLA Modules:
  0.0 678.4 jit_solution(5218221517429573839)
XLA Ops:
  8.0 7.2 %fusion.148 = f32[12288,128]{1,0:T(8,128)} fusion(bf16[12288,256]{1,0:T(8,128)(2,1)} %param.9, bf16[256,128]{1,0:T(8,128)(2,1)S(1)} %copy-done), kind=kOutput, calls=%fused_computation.157 | convolution fusion | flops 805306368 | bytes 12648448 | tf_op jit(solution)/shard_map/dot_general | solution.py:54
  17.4 168.0 %all-reduce.5.cloned.1.call-done = f32[48,256,128]{2,1,0:T(8,128)} async-done(((f32[48,256,128]{2,1,0:T(8,128)}), f32[48,256,128]{2,1,0:T(8,128)}) %all-reduce.5.cloned.1.call-update) | async-done | bytes 6291472 | tf_op jit(solution)/shard_map/psum | solution.py:55
  185.4 8.0 %multiply_reduce_fusion = (f32[48]{0:T(128)S(1)}, f32[48,256,128]{2,1,0:T(8,128)S(1)}) fusion(f32[128,128]{1,0:T(8,128)S(1)} %copy-done.2, f32[48,256,128]{2,1,0:T(8,128)} %all-reduce.5.cloned.1.call-done, f32[48,128]{1,0:T(8,128)S(1)} %fusion.143, f32[48,256]{1,0:T(8,128)S(1)} %fusion.103), kind=kOutput, calls=%fused_computation.9 | convolution fusion | flops 2422210560 | bytes 12722368 | tf_op jit(solution)/shard_map/bir,sr->bis/dot_general | solution.py:34
  193.7 11.1 %fusion.60 = f32[48,128,128]{2,1,0:T(8,128)S(1)} fusion(f32[48,256,128]{2,1,0:T(8,128)S(1)} %get-tuple-element.78, f32[48]{0:T(128)S(1)} %convolution_bitcast_fusion), kind=kOutput, calls=%fused_computation.60 | convolution fusion | flops 2417491968 | bytes 9437376 | tf_op jit(solution)/shard_map/bir,bis->brs/dot_general | solution.py:38
  204.7 3.2 fusion.41
  209.9 7.4 %fusion.39 = f32[48,256,128]{2,1,0:T(8,128)S(1)} fusion(f32[48,128,128]{2,0,1:T(8,128)S(1)} %fusion.75, f32[48,256,128]{2,1,0:T(8,128)S(1)} %get-tuple-element.78, f32[48]{0:T(128)S(1)} %convolution_bitcast_fusion), kind=kOutput, calls=%fused_computation.41 | convolution fusion | flops 2417491968 | bytes 15728832 | tf_op jit(solution)/shard_map/bir,brs->bis/dot_general | solution.py:44
  217.3 10.8 %fusion.149 = f32[48,128,128]{2,1,0:T(8,128)S(1)} fusion(f32[48,256,128]{2,1,0:T(8,128)S(1)} %fusion.39), kind=kOutput, calls=%fused_computation.158 | convolution fusion | flops 2415919104 | bytes 9437184 | tf_op jit(solution)/shard_map/bir,bis->brs/dot_general | solution.py:38
  228.1 3.2 fusion.37
  233.2 7.3 %fusion.35 = f32[48,256,128]{2,1,0:T(8,128)S(1)} fusion(f32[48,256,128]{2,1,0:T(8,128)S(1)} %fusion.39, f32[48,128,128]{2,0,1:T(8,128)S(1)} %fusion.73), kind=kOutput, calls=%fused_computation.37 | convolution fusion | flops 2415919104 | bytes 15728640 | tf_op jit(solution)/shard_map/bir,brs->bis/dot_general | solution.py:44
  240.5 10.6 %fusion.150 = f32[48,128,128]{2,1,0:T(8,128)S(1)} fusion(f32[48,256,128]{2,1,0:T(8,128)S(1)} %fusion.35), kind=kOutput, calls=%fused_computation.159 | convolution fusion | flops 2415919104 | bytes 9437184 | tf_op jit(solution)/shard_map/bir,bis->brs/dot_general | solution.py:38
  251.1 3.0 fusion.33
  254.5 2.0 fusion.71
  256.5 7.3 %fusion.31 = f32[48,256,128]{2,1,0:T(8,128)S(1)} fusion(f32[48,256,128]{2,1,0:T(8,128)S(1)} %fusion.35, f32[48,128,128]{2,0,1:T(8,128)S(1)} %fusion.71), kind=kOutput, calls=%fused_computation.33 | convolution fusion | flops 2415919104 | bytes 15728640 | tf_op jit(solution)/shard_map/bir,brs->bis/dot_general | solution.py:44
  263.8 10.6 %fusion.151 = f32[48,128,128]{2,1,0:T(8,128)S(1)} fusion(f32[48,256,128]{2,1,0:T(8,128)S(1)} %fusion.31), kind=kOutput, calls=%fused_computation.160 | convolution fusion | flops 2415919104 | bytes 9437184 | tf_op jit(solution)/shard_map/bir,bis->brs/dot_general | solution.py:38
  274.4 3.0 fusion.29
  279.3 7.5 %fusion.27 = f32[48,256,128]{2,1,0:T(8,128)S(1)} fusion(f32[48,256,128]{2,1,0:T(8,128)S(1)} %fusion.31, f32[48,128,128]{2,0,1:T(8,128)S(1)} %fusion.69), kind=kOutput, calls=%fused_computation.29 | convolution fusion | flops 2415919104 | bytes 15728640 | tf_op jit(solution)/shard_map/bir,brs->bis/dot_general | solution.py:44
  286.8 10.8 %fusion.152 = f32[48,128,128]{2,1,0:T(8,128)S(1)} fusion(f32[48,256,128]{2,1,0:T(8,128)S(1)} %fusion.27), kind=kOutput, calls=%fused_computation.161 | convolution fusion | flops 2415919104 | bytes 9437184 | tf_op jit(solution)/shard_map/bir,bis->brs/dot_general | solution.py:38
  297.6 3.0 fusion.25
  302.5 7.5 %fusion.23 = f32[48,256,128]{2,1,0:T(8,128)S(1)} fusion(f32[48,256,128]{2,1,0:T(8,128)S(1)} %fusion.27, f32[48,128,128]{2,0,1:T(8,128)S(1)} %fusion.67), kind=kOutput, calls=%fused_computation.25 | convolution fusion | flops 2415919104 | bytes 15728640 | tf_op jit(solution)/shard_map/bir,brs->bis/dot_general | solution.py:44
  310.0 10.6 %fusion.153 = f32[48,128,128]{2,1,0:T(8,128)S(1)} fusion(f32[48,256,128]{2,1,0:T(8,128)S(1)} %fusion.23), kind=kOutput, calls=%fused_computation.162 | convolution fusion | flops 2415919104 | bytes 9437184 | tf_op jit(solution)/shard_map/bir,bis->brs/dot_general | solution.py:38
  320.6 3.0 fusion.21
  325.6 7.7 %fusion.19 = f32[48,256,128]{2,1,0:T(8,128)S(1)} fusion(f32[48,256,128]{2,1,0:T(8,128)S(1)} %fusion.23, f32[48,128,128]{2,0,1:T(8,128)S(1)} %fusion.65), kind=kOutput, calls=%fused_computation.21 | convolution fusion | flops 2415919104 | bytes 15728640 | tf_op jit(solution)/shard_map/bir,brs->bis/dot_general | solution.py:44
  333.3 10.4 %fusion.154 = f32[48,128,128]{2,1,0:T(8,128)S(1)} fusion(f32[48,256,128]{2,1,0:T(8,128)S(1)} %fusion.19), kind=kOutput, calls=%fused_computation.163 | convolution fusion | flops 2415919104 | bytes 9437184 | tf_op jit(solution)/shard_map/bir,bis->brs/dot_general | solution.py:38
  343.7 3.2 fusion.17
  348.8 7.3 %fusion.15 = f32[48,256,128]{2,1,0:T(8,128)S(1)} fusion(f32[48,256,128]{2,1,0:T(8,128)S(1)} %fusion.19, f32[48,128,128]{2,0,1:T(8,128)S(1)} %fusion.63), kind=kOutput, calls=%fused_computation.17 | convolution fusion | flops 2415919104 | bytes 15728640 | tf_op jit(solution)/shard_map/bir,brs->bis/dot_general | solution.py:44
  356.1 10.6 %fusion.155 = f32[48,128,128]{2,1,0:T(8,128)S(1)} fusion(f32[48,256,128]{2,1,0:T(8,128)S(1)} %fusion.15), kind=kOutput, calls=%fused_computation.164 | convolution fusion | flops 2415919104 | bytes 9437184 | tf_op jit(solution)/shard_map/bir,bis->brs/dot_general | solution.py:38
  366.7 3.4 fusion.13
  372.0 7.8 %fusion.45 = bf16[48,256,128]{2,1,0:T(8,128)(2,1)} fusion(f32[48,256,128]{2,1,0:T(8,128)S(1)} %fusion.15, f32[48,128,128]{2,0,1:T(8,128)S(1)} %fusion.61), kind=kOutput, calls=%fused_computation.48 | convolution fusion | flops 2417491968 | bytes 12582912 | tf_op jit(solution)/shard_map/bir,brs->bis/dot_general | solution.py:44
  379.8 35.7 %while.11 = (s32[]{:T(128)}, f32[12,128,256]{2,0,1:T(8,128)S(1)}, s32[6]{0:T(128)S(1)}, f32[12,48]{0,1:T(8,128)S(1)}, bf16[48,256,128]{2,1,0:T(8,128)(2,1)}, /*i...) while((s32[]{:T(128)}, f32[12,128,256]{2,0,1:T(8,128)S(1)}, ...), condition=%wide.region_8.10_spmd.clone, body=%wide.region_7.9_spmd.clone.sunk | while | flops 172752896 | bytes 7345325 | solution.py:80
  382.8 2.9 select_add_fusion.2
  387.0 1.7 fusion.201
  388.7 2.9 select_add_fusion.2
  392.9 1.7 fusion.201
  394.6 2.9 select_add_fusion.2
  398.8 1.7 fusion.201
  400.6 2.9 select_add_fusion.2
  406.5 2.9 select_add_fusion.2
  410.7 1.7 fusion.201
  412.4 2.9 select_add_fusion.2
  415.5 3.9 fusion.54
  419.5 70.1 %all-reduce.9.cloned.1.call-done = (f32[256,128]{1,0:T(8,128)}, f32[128,128]{0,1:T(8,128)}) async-done(((f32[256,128]{1,0:T(8,128)}, f32[128,128]{0,1:T(8,128)}), (f32[256,128]{1,0:T(8,128)}, f32[128,128]{0,1:T(8,128)})) %all-reduce.9.cloned.1.call-update) | async-done | bytes 196624 | tf_op jit(solution)/shard_map/psum | solution.py:89
  490.9 11.7 %cholesky.44 = f32[128,128]{1,0:T(8,128)S(1)} custom-call(f32[128,128]{1,0:T(8,128)S(1)} %fusion.101), custom_call_target="Cholesky" | custom-call | tf_op jit(solution)/shard_map/jit(cholesky)/cholesky | solution.py:28
  503.9 9.8 %custom-call.16 = f32[1,128,128]{1,2,0:T(8,128)S(1)} custom-call(f32[1,128,128]{2,1,0:T(8,128)S(1)} %fusion.89), custom_call_target="InvertDiagBlocksLowerTriangular" | custom-call | tf_op jit(solution)/shard_map/jit(_cho_solve)/triangular_solve | solution.py:29
  516.2 2.2 fusion.51
  519.1 39.1 %psum.39 = f32[12,128]{1,0:T(8,128)S(1)} all-reduce(f32[12,128]{1,0:T(8,128)S(1)} %fusion.51), channel_id=1, replica_groups=mesh['run'=8,'mz'=16] {'mz'}, use_global_device_ids=true, to_apply=%region_12.14 | all-reduce | flops 1536 | bytes 12288 | tf_op jit(solution)/shard_map/psum | solution.py:94
  558.2 88.5 %all-reduce.7.cloned.1.call-done = f32[128,128]{0,1:T(8,128)} async-done(((f32[128,128]{0,1:T(8,128)}), f32[128,128]{0,1:T(8,128)}) %all-reduce.7.cloned.1.call-update) | async-done | bytes 65552 | tf_op jit(solution)/shard_map/psum | solution.py:94
  647.6 11.7 %cholesky.55 = f32[128,128]{1,0:T(8,128)S(1)} custom-call(f32[128,128]{1,0:T(8,128)S(1)} %fusion.95), custom_call_target="Cholesky" | custom-call | tf_op jit(solution)/shard_map/jit(cholesky)/cholesky | solution.py:28
  660.7 9.8 %custom-call.17 = f32[1,128,128]{1,2,0:T(8,128)S(1)} custom-call(f32[1,128,128]{2,1,0:T(8,128)S(1)} %fusion.90), custom_call_target="InvertDiagBlocksLowerTriangular" | custom-call | tf_op jit(solution)/shard_map/jit(_cho_solve)/triangular_solve | solution.py:29
  (72 shorter events, 33.0 us)
Async XLA Ops:
  7.2 0.8 copy-start
  7.2 178.2 %all-reduce.5.cloned.1.call-start = ((), (), s32[]{:S(2)}) async-start(), calls=%async_computation | async-start | bytes 12582912 | tf_op jit(solution)/shard_map/psum | solution.py:55
  15.2 0.7 copy-start.4
  15.3 0.9 copy-start.5
  15.3 1.0 copy-start.3
  15.3 170.1 %copy-start.2 = (f32[128,128]{1,0:T(8,128)S(1)}, f32[128,128]{1,0:T(8,128)}, u32[]{:S(2)}) copy-start(f32[128,128]{1,0:T(8,128)} %param.11) | copy-start | bytes 196612
  15.3 474.3 %all-reduce.9.cloned.1.call-start = ((), (), s32[]{:S(2)}) async-start(), calls=%async_computation.2 | async-start | bytes 393216 | tf_op jit(solution)/shard_map/psum | solution.py:89
  415.5 256.1 %copy-start.1 = (bf16[256,128]{1,0:T(8,128)(2,1)S(1)}, bf16[256,128]{1,0:T(8,128)(2,1)}, u32[]{:S(2)}) copy-start(bf16[256,128]{1,0:T(8,128)(2,1)} %param.10) | copy-start | bytes 196612
  419.5 227.2 %all-reduce.7.cloned.1.call-start = ((), (), s32[]{:S(2)}) async-start(), calls=%async_computation.1 | async-start | bytes 131072 | tf_op jit(solution)/shard_map/psum | solution.py:94
Sparse Core Ops, SparseCore 0:
  15.4 169.9 all-reduce.4
  419.6 69.9 all-reduce.8
  516.3 130.3 all-reduce.6
where the time goes:
time: 683 us; the launch traced here: 678 us
  waiting for transfers between devices  327 us (48%)
  matrix products  239 us (35%)
  other arithmetic  49.3 us (7%)
  blocking collectives  39.1 us (6%)
  between operations  14.4 us (2%)
    psum x1, waiting for transfers between devices, per_device(): scores = lax.psum(partial_value, 'mz')  168 us
    psum x1, waiting for transfers between devices, per_device(): equation, mz_gram = lax.psum((equation_part, mz_part), 'mz')  88.5 us
    dot_general x8, matrix products, run_gram(): block_grams = jnp.einsum('bir,bis->brs', values, values, precision=highest)  85.4 us
    psum x1, waiting for transfers between devices, per_device(): gathered, weight_gram = lax.psum((partial_terms, own_gram), 'run')  70.1 us
    dot_general x8, matrix products, apply_factors(): return jnp.einsum('bir,brs->bis', values, spread, precision=highest)  59.7 us
    psum x1, blocking collectives, per_device(): equation, mz_gram = lax.psum((equation_part, mz_part), 'mz')  39.1 us
    dot_general x8, matrix products, run_gram(): return jnp.einsum('kb,brs->krs', member, block_grams, precision=highest)  25 us
    another operation x6, other arithmetic, solve_right(): lower = jnp.linalg.cholesky(matrix)  24.8 us
  transfers between devices with their start and end apart: 3, of which 3 were waited for; matrix products, arithmetic and copies ran while one was open for 1% of the time, Pallas kernels for 0%

commit v1 on v0

v1 whole, which is shorter than its diff:
```python
import functools

import jax
import jax.numpy as jnp
from jax import lax
from jax.experimental import pallas as pl
from jax.experimental.pallas import tpu as pltpu
from jax.sharding import PartitionSpec as P

R = 128
BLOCK = 256
NSTEPS = 8
RUN_DEV = 12
SLOTS = 48
MAXB = 8
CHIPS = 8
N_RUN = 8
OWN = 3
TILES = 6
ROWS = TILES * R
CODED = ROWS + 16
WIDTH = 256
LEVELS = 32000.0
INV_STEPS = 26

MESH = pl.DeviceIdType.MESH
F32 = jnp.float32
BF16 = jnp.bfloat16


def split(x):
    hi = x.astype(BF16)
    return hi, (x - hi.astype(F32)).astype(BF16)


def mm(x, y):
    xh, xl = split(x)
    yh, yl = split(y)
    right = jnp.concatenate([yh, yl], axis=1)
    out = jnp.dot(
        jnp.concatenate([xh, xl], axis=1),
        jnp.concatenate([right, right], axis=0),
        preferred_element_type=F32,
    )
    return out[:, :R] + out[:, R:]


def mm_nt(x, y):
    xh, xl = split(x)
    yh, yl = split(y)
    right = jnp.concatenate(
        [jnp.concatenate([yh, yh], axis=1), jnp.concatenate([yl, yl], axis=1)], axis=0
    )
    out = lax.dot_general(
        jnp.concatenate([xh, xl], axis=1),
        right,
        (((1,), (1,)), ((), ())),
        preferred_element_type=F32,
    )
    return out[:, :R] + out[:, R:]


def stack_left(x):
    xh, xl = split(x)
    return jnp.concatenate(
        [jnp.concatenate([xh, xh], axis=1), jnp.concatenate([xl, xl], axis=1)], axis=0
    )


def wide(left, y):
    yh, yl = split(y)
    out = jnp.dot(left, jnp.concatenate([yh, yl], axis=0), preferred_element_type=F32)
    return out[:R] + out[R:]


def self_gram(x):
    xh, xl = split(x)
    both = jnp.concatenate([xh, xl], axis=0)
    out = lax.dot_general(both, both, (((1,), (1,)), ((), ())), preferred_element_type=F32)
    return out[:R, :R] + out[:R, R:] + out[R:, :R] + out[R:, R:]


def eye_mask():
    return lax.broadcasted_iota(jnp.int32, (R, R), 0) == lax.broadcasted_iota(jnp.int32, (R, R), 1)


def inverse_start(matrix):
    eye = eye_mask()
    diagonal = jnp.where(eye, matrix, 0.0)
    row = lax.rsqrt(jnp.sum(diagonal, axis=0, keepdims=True))
    column = lax.rsqrt(jnp.sum(diagonal, axis=1, keepdims=True))
    scaled = matrix * row * column
    bound = jnp.max(jnp.sum(jnp.abs(scaled), axis=0, keepdims=True), axis=1, keepdims=True)
    alpha = 1.0 / bound
    unit = jnp.where(eye, 1.0, 0.0)
    return scaled, row, column, alpha * unit, unit - alpha * scaled


def inverse_step(x, r):
    out = mm(jnp.concatenate([x, r], axis=0), r)
    return x + out[:R], out[R:]


def inverse_polish(scaled, x):
    residual = jnp.where(eye_mask(), 1.0, 0.0) - mm(scaled, x)
    return x + mm(x, residual)


def encode(x):
    top = jnp.max(jnp.max(jnp.abs(x), axis=0), axis=0, keepdims=True)
    code = jnp.ceil(jnp.log(jnp.maximum(top, 1e-30)) * 64.0)
    factor = jnp.exp(code * (-1.0 / 64.0)) * LEVELS
    return jnp.round(x * factor[None]).astype(jnp.int32).astype(jnp.int16), code


def decode_scale(code_rows):
    return jnp.exp(code_rows.astype(F32)[:1] * (1.0 / 64.0)) * (1.0 / LEVELS)


def main_kernel(
    x_hbm, v_ref, h_ref, w_ref, count_ref, trim_ref,
    nmt_ref, sums_ref,
    xv, vt, dsend, drecv, keep, rs_send, rs_recv, acc, agbuf, st, gram, gs, qs, ft, zb, us,
    wall, cinv, wt, bpart, brecv, ball, e_part, e_sib, e_half, e_recv, e_out, e_fin,
    xsem, d_s, d_r, rs_s, rs_r, ag_s, ag_r, fw_s, fw_r, w_s, w_r, b1_s, b1_r, b2_s, b2_r,
    e1_s, e1_r, e2_s, e2_r, e3_s, e3_r,
):
    run = lax.axis_index("run")
    me = lax.axis_index("mz")
    chip = lax.div(me, 2)
    core = lax.rem(me, 2)
    sibling = (run, chip * 2 + 1 - core)

    def chip_at(step):
        return lax.rem(chip + step, CHIPS)

    def peer(step):
        return (run, chip_at(step) * 2 + core)

    def run_peer(step):
        return (lax.rem(run + step, N_RUN), me)

    def x_copy(step, side):
        chunk = chip_at(step + 1) * 2 + (core if side else 1 - core)
        rows = pl.ds(pl.multiple_of(chunk * ROWS, ROWS), ROWS)
        return pltpu.make_async_copy(x_hbm.at[rows], xv.at[rows], xsem.at[step * 2 + side])

    for step in range(CHIPS):
        x_copy(step, 0).start()
        x_copy(step, 1).start()

    barrier = pltpu.get_barrier_semaphore()
    pl.semaphore_signal(barrier, inc=1, device_id=sibling, device_id_type=MESH)
    for step in range(1, CHIPS):
        pl.semaphore_signal(barrier, inc=1, device_id=peer(step), device_id_type=MESH)
        pl.semaphore_signal(barrier, inc=1, device_id=run_peer(step), device_id_type=MESH)

    vt[...] = v_ref[...].astype(F32).T.astype(BF16)
    weights = jnp.concatenate([w_ref[...], jnp.zeros((16 - RUN_DEV, R), F32)], axis=0)
    wall[run] = weights

    pl.semaphore_wait(barrier, 2 * CHIPS - 1)

    def send(src, dst, s_sem, r_sem, device):
        return pltpu.make_async_remote_copy(
            src_ref=src, dst_ref=dst, send_sem=s_sem, recv_sem=r_sem,
            device_id=device, device_id_type=MESH,
        )

    def run_from(step):
        return lax.rem(run + N_RUN - step, N_RUN)

    def chip_from(step):
        return lax.rem(chip + CHIPS - step, CHIPS)

    def w_copy(step, slot=run):
        return send(wall.at[slot], wall.at[slot], w_s.at[step], w_r.at[step], run_peer(step))

    for step in range(1, N_RUN):
        w_copy(step).start()

    def partial(chunk, dst, step):
        for i in range(OWN):
            rows = pl.ds(pl.multiple_of(chunk * ROWS + i * BLOCK, BLOCK), BLOCK)
            out = lax.dot_general(
                vt[...], xv[rows, :], (((1,), (1,)), ((), ())), preferred_element_type=F32
            )
            dst[step, 2 * i] = out[:, :R]
            dst[step, 2 * i + 1] = out[:, R:]

    def d_copy(step):
        return send(dsend.at[step], drecv.at[step], d_s.at[step], d_r.at[step], sibling)

    def rs_copy(step):
        return send(rs_send.at[step], rs_recv.at[step], rs_s.at[step], rs_r.at[step], peer(step + 1))

    def reduce_body(step, carry):
        @pl.when(step < CHIPS)
        def _():
            target = chip_at(step + 1)
            x_copy(step, 0).wait()
            partial(target * 2 + 1 - core, dsend, step)
            d_copy(step).start()
            x_copy(step, 1).wait()
            partial(target * 2 + core, keep, step)

        @pl.when((step >= 1) & (step < CHIPS))
        def _():
            last = step - 1
            d_copy(last).wait_recv()
            values, code = encode(keep[last] + drecv[last])
            rs_send[last, :ROWS] = values.reshape(ROWS, R)
            rs_send[last, ROWS:] = jnp.broadcast_to(code, (16, R)).astype(jnp.int32).astype(jnp.int16)
            rs_copy(last).start()

        return carry

    lax.fori_loop(0, CHIPS, reduce_body, 0)

    for step in range(1, N_RUN):
        w_copy(step, run_from(step)).wait_recv()
    all_weights = wall[...].reshape(N_RUN * 16, R)
    h = h_ref[...]
    ht = h.T
    mix_gram = mm(ht, h)
    c_matrix = mm(all_weights.T, all_weights) * mix_gram
    scaled, row, column, x0, r0 = inverse_start(c_matrix)

    def inv_body(i, carry):
        return inverse_step(*carry)

    x0, r0 = lax.fori_loop(0, INV_STEPS, inv_body, (x0, r0))
    x0 = inverse_polish(scaled, x0)
    x0 = inverse_polish(scaled, x0)
    cinv[...] = x0 * row * column
    own_weights = jnp.concatenate([weights, jnp.zeros((R - 16, R), F32)], axis=0)
    wt[...] = own_weights.T

    d_copy(CHIPS - 1).wait_recv()
    acc[...] = keep[CHIPS - 1] + drecv[CHIPS - 1]

    def sum_body(step, carry):
        rs_copy(step).wait_recv()
        scale = decode_scale(rs_recv[step, ROWS:])
        acc[...] += rs_recv[step, :ROWS].astype(F32).reshape(TILES, R, R) * scale[None]
        return carry

    lax.fori_loop(0, CHIPS - 1, sum_body, 0)

    starts = []
    total = jnp.int32(0)
    for k in range(RUN_DEV):
        starts.append(total)
        total = total + count_ref[0, k]
    ends = starts[1:] + [total]
    lane = lax.broadcasted_iota(jnp.int32, (1, R), 1)
    for i in range(OWN):
        block = me * OWN + i
        limit = jnp.int32(BLOCK)
        for k in range(RUN_DEV):
            limit = limit - jnp.where(block == ends[k] - 1, trim_ref[0, k], 0)
        acc[2 * i] = jnp.where(lane < limit, acc[2 * i], 0.0)
        acc[2 * i + 1] = jnp.where(lane + R < limit, acc[2 * i + 1], 0.0)

    values, code = encode(acc[...])
    agbuf[me, :ROWS] = values.reshape(ROWS, R)
    agbuf[me, ROWS:] = jnp.broadcast_to(code, (16, R)).astype(jnp.int32).astype(jnp.int16)

    def ag_copy(step, slot=me):
        return send(agbuf.at[slot], agbuf.at[slot], ag_s.at[step], ag_r.at[step], peer(step))

    def fw_copy(step, side=core):
        slot = chip_from(step) * 2 + side
        return send(agbuf.at[slot], agbuf.at[slot], fw_s.at[step], fw_r.at[step], sibling)

    for step in range(1, CHIPS):
        ag_copy(step).start()

    def take(slot):
        scale = decode_scale(agbuf[slot, ROWS:])
        for i in range(OWN):
            block = slot * OWN + i
            for t in range(2):
                rows = slice((2 * i + t) * R, (2 * i + t + 1) * R)
                hi, lo = split(agbuf[slot, rows].astype(F32) * scale)
                st[block, :R, t * R : (t + 1) * R] = hi
                st[block, R:, t * R : (t + 1) * R] = lo
            both = st[block]
            out = lax.dot_general(
                both, both, (((1,), (1,)), ((), ())), preferred_element_type=F32
            )
            gram[block] = (out[:R, :R] + out[R:, R:]) + (out[:R, R:] + out[R:, :R])

    def gather_body(step, carry):
        @pl.when((step >= 1) & (step < CHIPS))
        def _():
            ag_copy(step, chip_from(step) * 2 + core).wait_recv()

        @pl.when(step < CHIPS)
        def _():
            fw_copy(step).start()
            take(chip_from(step) * 2 + core)

        @pl.when(step >= 1)
        def _():
            last = step - 1
            fw_copy(last, 1 - core).wait_recv()
            take(chip_from(last) * 2 + 1 - core)

        return carry

    lax.fori_loop(0, CHIPS + 1, gather_body, 0)

    h = h_ref[...]
    eye = eye_mask()
    unit = jnp.where(eye, 1.0, 0.0)

    def first_body(k, start):
        count = count_ref[0, k]
        s = gram[jnp.minimum(start, SLOTS - 1)]
        for i in range(1, MAXB):
            s = s + jnp.where(i < count, gram[jnp.minimum(start + i, SLOTS - 1)], 0.0)
        left = h * w_ref[pl.ds(k, 1), :]
        g = mm_nt(mm(left, s), left)
        square = jnp.sum(jnp.sum(jnp.where(eye, g, 0.0), axis=0, keepdims=True), axis=1, keepdims=True)
        inv_norm = lax.rsqrt(square + 1e-6)
        g = g * (inv_norm * inv_norm)
        gs[k] = g
        qs[k] = unit * inv_norm
        return start + count

    lax.fori_loop(0, RUN_DEV, first_body, jnp.int32(0))

    def newton_body(i, carry):
        def group(j, inner):
            for u in range(4):
                k = j * 4 + u
                g = gs[k]
                c = 1.5 * unit - 0.5 * g
                out = mm(jnp.concatenate([g, qs[k]], axis=0), c)
                qs[k] = out[R:]
                gs[k] = mm(out[:R], c)
            return inner

        return lax.fori_loop(0, RUN_DEV // 4, group, carry)

    lax.fori_loop(0, NSTEPS - 1, newton_body, 0)

    def last_body(k, carry):
        c = 1.5 * unit - 0.5 * gs[k]
        left = h * w_ref[pl.ds(k, 1), :]
        ft[k] = stack_left(mm(mm(qs[k], c), left))
        return carry

    lax.fori_loop(0, RUN_DEV, last_body, 0)

    def project_body(block, carry):
        owner = jnp.int32(0)
        end = jnp.int32(0)
        for k in range(RUN_DEV - 1):
            end = end + count_ref[0, k]
            owner = owner + jnp.where(block >= end, 1, 0)
        out = jnp.dot(ft[owner], st[block], preferred_element_type=F32)
        polar = (out[:R] + out[R:]).astype(BF16)
        rows = pl.ds(pl.multiple_of(block * BLOCK, BLOCK), BLOCK)
        zb[block] = jnp.dot(polar, xv[rows, :], preferred_element_type=F32)
        return carry

    lax.fori_loop(0, SLOTS, project_body, 0)

    left_h = stack_left(h.T)
    bpart[...] = jnp.zeros_like(bpart)
    wcols = wt[...]

    def combine_body(k, start):
        count = count_ref[0, k]
        z = zb[jnp.minimum(start, SLOTS - 1)]
        for i in range(1, MAXB):
            z = z + jnp.where(i < count, zb[jnp.minimum(start + i, SLOTS - 1)], 0.0)
        u = wide(left_h, z)
        us[k] = u
        col = jnp.sum(
            jnp.where(lax.broadcasted_iota(jnp.int32, (R, R), 1) == k, wcols, 0.0), axis=1, keepdims=True
        )
        bpart[...] += (u * col).reshape(N_RUN, R // N_RUN, WIDTH)
        return start + count

    lax.fori_loop(0, RUN_DEV, combine_body, jnp.int32(0))

    def b1_copy(step):
        return send(
            bpart.at[lax.rem(run + step, N_RUN)], brecv.at[step], b1_s.at[step], b1_r.at[step], run_peer(step)
        )

    def b2_copy(step, slot=run):
        return send(ball.at[slot], ball.at[slot], b2_s.at[step], b2_r.at[step], run_peer(step))

    for step in range(1, N_RUN):
        b1_copy(step).start()
    own = bpart[run]
    for step in range(1, N_RUN):
        b1_copy(step).wait_recv()
        own = own + brecv[step]
    ball[run] = own
    for step in range(1, N_RUN):
        b2_copy(step).start()
    for step in range(1, N_RUN):
        b2_copy(step, run_from(step)).wait_recv()

    nmt = wide(stack_left(cinv[...]), ball[...].reshape(R, WIDTH))
    nmt_ref[...] = nmt

    e_part[:R] = self_gram(nmt)
    columns = jnp.zeros((R, R), F32)
    lanes = lax.broadcasted_iota(jnp.int32, (R, R), 1)
    for k in range(RUN_DEV):
        col = jnp.sum(us[k] * nmt, axis=1, keepdims=True)
        columns = jnp.where(lanes == k, col, columns)
    e_part[R:] = columns.T[:16]

    HALF = (R + 16) // 2
    e1 = send(e_part, e_sib, e1_s, e1_r, sibling)
    e1.start()
    e1.wait_recv()
    mine = pl.ds(pl.multiple_of(core * HALF, 8), HALF)
    e_half[...] = e_part[mine] + e_sib[mine]

    def e2_copy(step, slot=chip):
        return send(e_half, e_recv.at[slot], e2_s.at[step], e2_r.at[step], peer(step))

    for step in range(1, CHIPS):
        e2_copy(step).start()
    e_recv[chip] = e_half[...]
    for step in range(1, CHIPS):
        e2_copy(step, chip_from(step)).wait_recv()
    e_out[...] = jnp.sum(e_recv[...], axis=0)
    e3 = send(e_out, e_fin, e3_s, e3_r, sibling)
    e3.start()
    sums_ref[mine] = e_out[...]
    e3.wait_recv()
    other = pl.ds(pl.multiple_of((1 - core) * HALF, 8), HALF)
    sums_ref[other] = e_fin[...]

    for step in range(1, N_RUN):
        w_copy(step).wait_send()
        b1_copy(step).wait_send()
        b2_copy(step).wait_send()
    for step in range(1, CHIPS):
        rs_copy(step - 1).wait_send()
        ag_copy(step).wait_send()
        e2_copy(step).wait_send()
    for step in range(CHIPS):
        d_copy(step).wait_send()
        fw_copy(step).wait_send()
    e1.wait_send()
    e3.wait_send()


def last_kernel(nmt_ref, sums_ref, h_ref, nm_ref, nw_ref):
    nm_ref[...] = nmt_ref[...].T
    h = h_ref[...]
    matrix = sums_ref[:R] * mm(h.T, h)
    scaled, row, column, x, r = inverse_start(matrix)

    def more(carry):
        step, x, r = carry
        return (step < 10) & (jnp.max(jnp.abs(r)) > 1e-6)

    def body(carry):
        step, x, r = carry
        for _ in range(4):
            x, r = inverse_step(x, r)
        return step + 1, x, r

    _, x, r = lax.while_loop(more, body, (jnp.int32(0), x, r))
    x = inverse_polish(scaled, x)
    nw_ref[...] = mm(sums_ref[R:], x * row * column)[:RUN_DEV]


def per_device(spectra, mz_factor, mixing, run_weights, block_count, trim_scans):
    vmem = pl.BlockSpec(memory_space=pltpu.VMEM)
    smem = pl.BlockSpec(memory_space=pltpu.SMEM)
    dma8 = pltpu.SemaphoreType.DMA((8,))
    dma = pltpu.SemaphoreType.DMA
    half = (R + 16) // 2
    nmt, sums = pl.pallas_call(
        main_kernel,
        out_shape=(
            jax.ShapeDtypeStruct((R, WIDTH), F32),
            jax.ShapeDtypeStruct((R + 16, R), F32),
        ),
        in_specs=[pl.BlockSpec(memory_space=pl.ANY), vmem, vmem, vmem, smem, smem],
        out_specs=(vmem, vmem),
        scratch_shapes=[
            pltpu.VMEM((SLOTS * BLOCK, WIDTH), BF16),
            pltpu.VMEM((R, WIDTH), BF16),
            pltpu.VMEM((CHIPS, TILES, R, R), F32),
            pltpu.VMEM((CHIPS, TILES, R, R), F32),
            pltpu.VMEM((CHIPS, TILES, R, R), F32),
            pltpu.VMEM((CHIPS - 1, CODED, R), jnp.int16),
            pltpu.VMEM((CHIPS - 1, CODED, R), jnp.int16),
            pltpu.VMEM((TILES, R, R), F32),
            pltpu.VMEM((2 * CHIPS, CODED, R), jnp.int16),
            pltpu.VMEM((SLOTS, 2 * R, BLOCK), BF16),
            pltpu.VMEM((SLOTS, R, R), F32),
            pltpu.VMEM((RUN_DEV, R, R), F32),
            pltpu.VMEM((RUN_DEV, R, R), F32),
            pltpu.VMEM((RUN_DEV, 2 * R, 2 * R), BF16),
            pltpu.VMEM((SLOTS, R, WIDTH), F32),
            pltpu.VMEM((RUN_DEV, R, WIDTH), F32),
            pltpu.VMEM((N_RUN, 16, R), F32),
            pltpu.VMEM((R, R), F32),
            pltpu.VMEM((R, R), F32),
            pltpu.VMEM((N_RUN, R // N_RUN, WIDTH), F32),
            pltpu.VMEM((N_RUN, R // N_RUN, WIDTH), F32),
            pltpu.VMEM((N_RUN, R // N_RUN, WIDTH), F32),
            pltpu.VMEM((R + 16, R), F32),
            pltpu.VMEM((R + 16, R), F32),
            pltpu.VMEM((half, R), F32),
            pltpu.VMEM((CHIPS, half, R), F32),
            pltpu.VMEM((half, R), F32),
            pltpu.VMEM((half, R), F32),
            dma((2 * CHIPS,)),
            dma8, dma8, dma8, dma8, dma8, dma8, dma8, dma8,
            dma8, dma8, dma8, dma8, dma8, dma8,
            dma, dma, dma8, dma8, dma, dma,
        ],
        compiler_params=pltpu.CompilerParams(
            collective_id=0, has_side_effects=True, vmem_limit_bytes=58 * 2**20
        ),
    )(spectra, mz_factor, mixing, run_weights, block_count, trim_scans)
    return pl.pallas_call(
        last_kernel,
        out_shape=(
            jax.ShapeDtypeStruct((WIDTH, R), F32),
            jax.ShapeDtypeStruct((RUN_DEV, R), F32),
        ),
        in_specs=[vmem, vmem, vmem],
        out_specs=(vmem, vmem),
    )(nmt, sums, mixing)


def solution(mesh):
    placed = (P("run", "mz"), P("mz", None), P(), P("run", None), P("run", None), P("run", None))
    return jax.shard_map(
        per_device,
        mesh=mesh,
        in_specs=placed,
        out_specs=(P("mz", None), P("run", None)),
        check_vma=False,
    )
```

time: 683 us -> 128 us (0.19)
  waiting for transfers between devices: 327 us -> 0 us
  matrix products: 239 us -> 0 us
  Pallas kernels: 0 us -> 128 us
  other arithmetic: 49.3 us -> 0 us
  blocking collectives: 39.1 us -> 0 us
  between operations: 14.4 us -> 0.64 us
    psum x3 -> x0, waiting for transfers between devices: 327 us -> none  [the longest x1 168 us: per_device(): scores = lax.psum(partial_value, 'mz')]
    dot_general x54 -> x0, matrix products: 236 us -> none  [the longest x8 85.4 us: run_gram(): block_grams = jnp.einsum('bir,bis->brs', values, values, precision=highest)]
    pallas_call x0 -> x2, Pallas kernels: none -> 128 us  [the longest x1 123 us: per_device(): pl.pallas_call(main_kernel, out_shape=(jax.ShapeDtypeStruct((R, WIDTH), F...]
    another operation x11 -> x0, other arithmetic: 45.9 us -> none  [the longest x6 24.8 us: solve_right(): lower = jnp.linalg.cholesky(matrix)]
    psum x1 -> x0, blocking collectives: 39.1 us -> none  [per_device(): equation, mz_gram = lax.psum((equation_part, mz_part), 'mz')]
  transfers between devices with their start and end apart: 3 -> 0, of which waited for: 3 -> 0; matrix products, arithmetic and copies ran while one was open for 1% -> 0% of each run, Pallas kernels for 0% -> 0%
where the time goes in v1:
time: 128 us
  Pallas kernels  128 us (100%)
    pallas_call x1, Pallas kernels, per_device(): pl.pallas_call(main_kernel, out_shape=(jax.ShapeDtypeStruct((R, WIDTH), F...  123 us
    pallas_call x1, Pallas kernels, per_device(): pl.pallas_call(last_kernel, out_shape=(jax.ShapeDtypeStruct((WIDTH, R), F...  4.48 us

profile of v1, /device:TPU:1, one launch (start us, length us, event | category | flops | bytes accessed | tf_op | source)
XLA Modules:
  0.0 128.2 jit_solution(3557301206194623023)
XLA Ops:
  0.6 123.0 %shard_map.77 = (f32[128,256]{1,0:T(8,128)}, f32[144,128]{1,0:T(8,128)}) custom-call(bf16[12288,256]{1,0:T(8,128)(2,1)} %x_hbm.1, bf16[256,128]{1,0:T(8,128)(2,1)} %v_ref.1, f32[128,128]{1,0:T(8,128)} %h_ref.3, f32[12,128]{1,0:T(8,128)} %w_ref.1, s32[1,12]{1,0:T(1,128)} %count_ref.1, s32[1,12]{1,0:T(1,128)} %trim_ref.1), custom_call_target="tpu_custom_call" | custom-call | tf_op jit(solution)/shard_map/pallas_call | solution.py:486
  123.7 4.5 %shard_map.78 = (f32[256,128]{1,0:T(8,128)}, f32[12,128]{1,0:T(8,128)}) custom-call(f32[128,256]{1,0:T(8,128)} %get-tuple-element.4.nmt_ref, f32[144,128]{1,0:T(8,128)} %get-tuple-element.5.sums_ref, f32[128,128]{1,0:T(8,128)} %h_ref.3), custom_call_target="tpu_custom_call" | custom-call | tf_op jit(solution)/shard_map/pallas_call | solution.py:532

commit v2 on v1

v2 whole, which is shorter than its diff:
```python
import functools

import jax
import jax.numpy as jnp
from jax import lax
from jax.experimental import pallas as pl
from jax.experimental.pallas import tpu as pltpu
from jax.sharding import PartitionSpec as P

R = 128
BLOCK = 256
NSTEPS = 8
RUN_DEV = 12
SLOTS = 48
MAXB = 8
CHIPS = 8
N_RUN = 8
OWN = 3
PIECES = CHIPS * OWN
PIECE = BLOCK
CODED = PIECE + 16
WIDTH = 256
LEVELS = 32000.0
INV_STEPS = (4, 11, 11)

PAIR_RUNS = RUN_DEV // 2

OFFSETS = ((1, 0), (3, 0), (0, 1), (2, 0), (1, 1), (3, 1), (2, 1))

MESH = pl.DeviceIdType.MESH
F32 = jnp.float32
BF16 = jnp.bfloat16


def split(x):
    hi = x.astype(BF16)
    return hi, (x - hi.astype(F32)).astype(BF16)


def right_of(y):
    yh, yl = split(y)
    right = jnp.concatenate([yh, yl], axis=1)
    return jnp.concatenate([right, right], axis=0)


def times(x, right):
    xh, xl = split(x)
    out = jnp.dot(jnp.concatenate([xh, xl], axis=1), right, preferred_element_type=F32)
    return out[:, :R] + out[:, R:]


def mm(x, y):
    return times(x, right_of(y))


def mm_nt(x, y):
    xh, xl = split(x)
    yh, yl = split(y)
    right = jnp.concatenate(
        [jnp.concatenate([yh, yh], axis=1), jnp.concatenate([yl, yl], axis=1)], axis=0
    )
    out = lax.dot_general(
        jnp.concatenate([xh, xl], axis=1),
        right,
        (((1,), (1,)), ((), ())),
        preferred_element_type=F32,
    )
    return out[:, :R] + out[:, R:]


def stack_left(x):
    xh, xl = split(x)
    return jnp.concatenate(
        [jnp.concatenate([xh, xh], axis=1), jnp.concatenate([xl, xl], axis=1)], axis=0
    )


def wide(left, y):
    yh, yl = split(y)
    out = jnp.dot(left, jnp.concatenate([yh, yl], axis=0), preferred_element_type=F32)
    return out[:R] + out[R:]


def self_gram(x):
    xh, xl = split(x)
    both = jnp.concatenate([xh, xl], axis=0)
    out = lax.dot_general(both, both, (((1,), (1,)), ((), ())), preferred_element_type=F32)
    return out[:R, :R] + out[:R, R:] + out[R:, :R] + out[R:, R:]


def eye_mask():
    return lax.broadcasted_iota(jnp.int32, (R, R), 0) == lax.broadcasted_iota(jnp.int32, (R, R), 1)


def inverse_start(matrix):
    eye = eye_mask()
    diagonal = jnp.where(eye, matrix, 0.0)
    row = lax.rsqrt(jnp.sum(diagonal, axis=0, keepdims=True))
    column = lax.rsqrt(jnp.sum(diagonal, axis=1, keepdims=True))
    scaled = matrix * row * column
    bound = jnp.max(jnp.sum(jnp.abs(scaled), axis=0, keepdims=True), axis=1, keepdims=True)
    alpha = 1.0 / bound
    unit = jnp.where(eye, 1.0, 0.0)
    return scaled, row, column, alpha * unit, unit - alpha * scaled


def inverse_step(x, r):
    out = mm(jnp.concatenate([x, r], axis=0), r)
    return x + out[:R], out[R:]


def inverse_polish(scaled, x):
    residual = jnp.where(eye_mask(), 1.0, 0.0) - mm(scaled, x)
    return x + mm(x, residual)


def encode(x, dst):
    top = jnp.max(jnp.abs(x), axis=0, keepdims=True)
    code = jnp.ceil(jnp.log(jnp.maximum(top, 1e-30)) * 64.0)
    factor = jnp.exp(code * (-1.0 / 64.0)) * LEVELS
    dst[:PIECE] = jnp.round(x * factor).astype(jnp.int32).astype(jnp.int16)
    dst[PIECE:] = jnp.broadcast_to(code, (16, R)).astype(jnp.int32).astype(jnp.int16)


def decode(src):
    scale = decode_scale(src[PIECE:])
    return src[:PIECE].astype(F32) * scale


def decode_scale(code_rows):
    return jnp.exp(code_rows.astype(F32)[:1] * (1.0 / 64.0)) * (1.0 / LEVELS)


def main_kernel(
    x_hbm, v_ref, h_ref, w_ref, count_ref, trim_ref,
    nmt_ref, sums_ref,
    xv, dsend, drecv, keep, rs_send, rs_recv, acc, agbuf, st, gram, gs, qs, f_own, f_sib, ft, zb, us,
    wall, cinv, wt, bpart, brecv, ball, e_part, e_sib, e_half, e_recv, e_out, e_fin,
    xsem, d_s, d_r, rs_s, rs_r, ag_s, ag_r, fw_s, fw_r, w_s, w_r, b1_s, b1_r, b2_s, b2_r,
    e1_s, e1_r, e2_s, e2_r, e3_s, e3_r, f_s, f_r,
):
    run = lax.axis_index("run")
    me = lax.axis_index("mz")
    chip = lax.div(me, 2)
    core = lax.rem(me, 2)
    sibling = (run, chip * 2 + 1 - core)

    def chip_at(step):
        return lax.rem(chip + step, CHIPS)

    def peer(step):
        return (run, chip_at(step) * 2 + core)

    def run_peer(step):
        return (lax.rem(run + step, N_RUN), me)

    def x_chunk(step, side):
        return chip_at(step + 1) * 2 + (core if side else 1 - core)

    def x_copy(step, side):
        rows = pl.ds(pl.multiple_of(x_chunk(step, side) * OWN * BLOCK, BLOCK), OWN * BLOCK)
        return pltpu.make_async_copy(x_hbm.at[rows], xv.at[rows], xsem.at[step * 2 + side])

    for step in range(CHIPS):
        x_copy(step, 0).start()
        x_copy(step, 1).start()

    barrier = pltpu.get_barrier_semaphore()
    pl.semaphore_signal(barrier, inc=1, device_id=sibling, device_id_type=MESH)
    for step in range(1, CHIPS):
        pl.semaphore_signal(barrier, inc=1, device_id=peer(step), device_id_type=MESH)
        pl.semaphore_signal(barrier, inc=1, device_id=run_peer(step), device_id_type=MESH)

    weights = jnp.concatenate([w_ref[...], jnp.zeros((16 - RUN_DEV, R), F32)], axis=0)
    wall[run] = weights

    def partial_body(step, carry):
        x_copy(step, 0).wait()
        x_copy(step, 1).wait()
        for i in range(OWN):
            t = i * CHIPS + step
            outs = []
            for side in range(2):
                first = pl.multiple_of((x_chunk(step, side) * OWN + i) * BLOCK, BLOCK)
                outs.append(
                    jnp.dot(xv[pl.ds(first, BLOCK), :], v_ref[...], preferred_element_type=F32)
                )
            encode(outs[0], dsend.at[t])
            keep[t] = outs[1]
        return carry

    lax.fori_loop(0, CHIPS, partial_body, 0)

    pl.semaphore_wait(barrier, 2 * CHIPS - 1)

    def send(src, dst, s_sem, r_sem, device):
        return pltpu.make_async_remote_copy(
            src_ref=src, dst_ref=dst, send_sem=s_sem, recv_sem=r_sem,
            device_id=device, device_id_type=MESH,
        )

    def run_from(step):
        return lax.rem(run + N_RUN - step, N_RUN)

    def chip_from(step):
        return lax.rem(chip + CHIPS - step, CHIPS)

    def w_copy(step, slot=run):
        return send(wall.at[slot], wall.at[slot], w_s.at[step], w_r.at[step], run_peer(step))

    def d_copy(t):
        return send(dsend.at[t], drecv.at[t], d_s.at[t], d_r.at[t], sibling)

    def rs_copy(t):
        return send(rs_send.at[t], rs_recv.at[t], rs_s.at[t], rs_r.at[t], peer(lax.rem(t, CHIPS) + 1))

    def d_body(t, carry):
        d_copy(t).start()
        return carry

    lax.fori_loop(0, PIECES, d_body, 0)

    def reduce_body(b, carry):
        first = b * CHIPS
        for i in range(CHIPS):
            d_copy(first + i).wait_recv()
        for i in range(CHIPS - 1):
            t = first + i
            encode(keep[t] + decode(drecv.at[t]), rs_send.at[t])
        for i in range(CHIPS - 1):
            rs_copy(first + i).start()
        t = first + CHIPS - 1
        acc[b] = keep[t] + decode(drecv.at[t])
        return carry

    lax.fori_loop(0, OWN, reduce_body, 0)

    for step in range(1, N_RUN):
        w_copy(step).start()

    for step in range(1, N_RUN):
        w_copy(step, run_from(step)).wait_recv()
    all_weights = wall[...].reshape(N_RUN * 16, R)
    h = h_ref[...]
    ht = h.T
    mix_gram = mm(ht, h)
    c_matrix = mm(all_weights.T, all_weights) * mix_gram
    scaled, row, column, x0, r0 = inverse_start(c_matrix)

    def inv_body(i, carry):
        return inverse_step(*carry)

    own_weights = jnp.concatenate([weights, jnp.zeros((R - 16, R), F32)], axis=0)
    wt[...] = own_weights.T

    starts = []
    total = jnp.int32(0)
    for k in range(RUN_DEV):
        starts.append(total)
        total = total + count_ref[0, k]
    ends = starts[1:] + [total]
    scans = lax.broadcasted_iota(jnp.int32, (BLOCK, R), 0)

    def shifted(offset, sign):
        dz, dx = offset
        z = lax.rem(lax.div(chip, 2) + 4 + sign * dz, 4)
        return z * 2 + lax.rem(lax.rem(chip, 2) + dx, 2)

    def ag_copy(i, b, slot=me):
        device = (run, shifted(OFFSETS[i], 1) * 2 + core)
        part = agbuf.at[slot, b]
        return send(part, part, ag_s.at[i * OWN + b], ag_r.at[i * OWN + b], device)

    def source(i):
        return chip if i == CHIPS - 1 else shifted(OFFSETS[i], -1)

    def fw_copy(i, b, side=core):
        part = agbuf.at[source(i) * 2 + side, b]
        return send(part, part, fw_s.at[i * OWN + b], fw_r.at[i * OWN + b], sibling)

    def unpack(slot, b):
        block = slot * OWN + b
        values = decode(agbuf.at[slot, b])
        hi0, lo0 = split(values[:R])
        hi1, lo1 = split(values[R:])
        both = jnp.concatenate(
            [jnp.concatenate([hi0, hi1], axis=1), jnp.concatenate([lo0, lo1], axis=1)], axis=0
        )
        st[block] = both
        return block, both

    def take_pair(i, b):
        fw_copy(i, b, 1 - core).wait_recv()
        pair = [unpack(source(i) * 2 + side, b) for side in (core, 1 - core)]
        for block, both in pair:
            out = lax.dot_general(both, both, (((1,), (1,)), ((), ())), preferred_element_type=F32)
            gram[block] = (out[:R, :R] + out[R:, R:]) + (out[:R, R:] + out[R:, :R])

    for b in range(OWN):
        x0, r0 = lax.fori_loop(0, INV_STEPS[b], inv_body, (x0, r0))
        if b == OWN - 1:
            x0 = inverse_polish(scaled, x0)
            x0 = inverse_polish(scaled, x0)
            cinv[...] = x0 * row * column
        own = acc[b]
        for i in range(CHIPS - 1):
            rs_copy(b * CHIPS + i).wait_recv()
        for i in range(CHIPS - 1):
            own = own + decode(rs_recv.at[b * CHIPS + i])
        block = me * OWN + b
        limit = jnp.int32(BLOCK)
        for k in range(RUN_DEV):
            limit = limit - jnp.where(block == ends[k] - 1, trim_ref[0, k], 0)
        own = jnp.where(scans < limit, own, 0.0)
        encode(jnp.concatenate([own[:R].T, own[R:].T], axis=0), agbuf.at[me, b])
        for i in range(CHIPS - 1):
            ag_copy(i, b).start()
        fw_copy(CHIPS - 1, b).start()

    late = []
    for b in range(OWN):
        take_pair(CHIPS - 1, b)
    for b in range(OWN):
        for i in range(CHIPS - 1):
            ag_copy(i, b, source(i) * 2 + core).wait_recv()
            fw_copy(i, b).start()
            if late:
                take_pair(*late.pop())
            late.append((i, b))
    take_pair(*late.pop())

    h = h_ref[...]
    eye = eye_mask()
    unit = jnp.where(eye, 1.0, 0.0)

    first_run = core * PAIR_RUNS
    pair_runs = range(PAIR_RUNS)
    lefts, sums = [], []
    for j in pair_runs:
        k = first_run + j
        count = count_ref[0, k]
        start = jnp.int32(0)
        for i in range(RUN_DEV - 1):
            start = start + jnp.where(i < k, count_ref[0, i], 0)
        s = gram[jnp.minimum(start, SLOTS - 1)]
        for i in range(1, MAXB):
            s = s + jnp.where(i < count, gram[jnp.minimum(start + i, SLOTS - 1)], 0.0)
        sums.append(s)
        lefts.append(h * w_ref[pl.ds(k, 1), :])
    halves = [mm(lefts[j], sums[j]) for j in pair_runs]
    grams = [mm_nt(halves[j], lefts[j]) for j in pair_runs]
    for j in pair_runs:
        g = grams[j]
        square = jnp.sum(jnp.sum(jnp.where(eye, g, 0.0), axis=0, keepdims=True), axis=1, keepdims=True)
        inv_norm = lax.rsqrt(square + 1e-6)
        gs[j] = g * (inv_norm * inv_norm)
        qs[j] = unit * inv_norm

    def newton_body(i, carry):
        rights = [right_of(1.5 * unit - 0.5 * gs[j]) for j in pair_runs]
        outs = [times(gs[j], rights[j]) for j in pair_runs]
        news = [times(outs[j], rights[j]) for j in pair_runs]
        products = [times(qs[j], rights[j]) for j in pair_runs]
        for j in pair_runs:
            gs[j] = news[j]
            qs[j] = products[j]
        return carry

    lax.fori_loop(0, NSTEPS - 1, newton_body, 0)

    lasts = [mm(qs[j], 1.5 * unit - 0.5 * gs[j]) for j in pair_runs]
    lasts = [mm(lasts[j], h * w_ref[pl.ds(first_run + j, 1), :]) for j in pair_runs]
    for j in pair_runs:
        hi, lo = split(lasts[j])
        f_own[j, :R] = hi
        f_own[j, R:] = lo

    f_copy = send(f_own, f_sib, f_s, f_r, sibling)
    f_copy.start()
    for j in pair_runs:
        ft[first_run + j] = f_own[j]
    f_copy.wait_recv()
    for j in pair_runs:
        ft[PAIR_RUNS - first_run + j] = f_sib[j]

    def project(group):
        polars = []
        for u in range(8):
            block = group * 8 + u
            owner = jnp.int32(0)
            end = jnp.int32(0)
            for k in range(RUN_DEV - 1):
                end = end + count_ref[0, k]
                owner = owner + jnp.where(block >= end, 1, 0)
            factor = ft[owner]
            out = jnp.dot(
                jnp.concatenate([factor, factor], axis=1), st[block], preferred_element_type=F32
            )
            polars.append((out[:R] + out[R:]).astype(BF16))
        for u in range(8):
            block = group * 8 + u
            rows = slice(block * BLOCK, (block + 1) * BLOCK)
            zb[block] = jnp.dot(polars[u], xv[rows, :], preferred_element_type=F32)

    for group in range(SLOTS // 8):
        project(group)

    left_h = stack_left(h.T)
    bpart[...] = jnp.zeros_like(bpart)
    wcols = wt[...]

    def combine_one(k, start):
        count = count_ref[0, k]
        z = zb[jnp.minimum(start, SLOTS - 1)]
        for i in range(1, MAXB):
            z = z + jnp.where(i < count, zb[jnp.minimum(start + i, SLOTS - 1)], 0.0)
        u = wide(left_h, z)
        us[k] = u
        col = jnp.sum(
            jnp.where(lax.broadcasted_iota(jnp.int32, (R, R), 1) == k, wcols, 0.0), axis=1, keepdims=True
        )
        bpart[...] += (u * col).reshape(N_RUN, R // N_RUN, WIDTH)
        return start + count

    start = jnp.int32(0)
    for k in range(RUN_DEV):
        start = combine_one(k, start)

    def b1_copy(step):
        return send(
            bpart.at[lax.rem(run + step, N_RUN)], brecv.at[step], b1_s.at[step], b1_r.at[step], run_peer(step)
        )

    def b2_copy(step, slot=run):
        return send(ball.at[slot], ball.at[slot], b2_s.at[step], b2_r.at[step], run_peer(step))

    for step in range(1, N_RUN):
        b1_copy(step).start()
    own = bpart[run]
    for step in range(1, N_RUN):
        b1_copy(step).wait_recv()
        own = own + brecv[step]
    ball[run] = own
    for step in range(1, N_RUN):
        b2_copy(step).start()
    for step in range(1, N_RUN):
        b2_copy(step, run_from(step)).wait_recv()

    nmt = wide(stack_left(cinv[...]), ball[...].reshape(R, WIDTH))
    nmt_ref[...] = nmt

    e_part[:R] = self_gram(nmt)
    columns = jnp.zeros((R, R), F32)
    lanes = lax.broadcasted_iota(jnp.int32, (R, R), 1)
    for k in range(RUN_DEV):
        col = jnp.sum(us[k] * nmt, axis=1, keepdims=True)
        columns = jnp.where(lanes == k, col, columns)
    e_part[R:] = columns.T[:16]

    HALF = (R + 16) // 2
    e1 = send(e_part, e_sib, e1_s, e1_r, sibling)
    e1.start()
    e1.wait_recv()
    mine = pl.ds(pl.multiple_of(core * HALF, 8), HALF)
    e_half[...] = e_part[mine] + e_sib[mine]

    def e2_copy(step, slot=chip):
        return send(e_half, e_recv.at[slot], e2_s.at[step], e2_r.at[step], peer(step))

    for step in range(1, CHIPS):
        e2_copy(step).start()
    e_recv[chip] = e_half[...]
    for step in range(1, CHIPS):
        e2_copy(step, chip_from(step)).wait_recv()
    e_out[...] = jnp.sum(e_recv[...], axis=0)
    e3 = send(e_out, e_fin, e3_s, e3_r, sibling)
    e3.start()
    sums_ref[mine] = e_out[...]
    e3.wait_recv()
    other = pl.ds(pl.multiple_of((1 - core) * HALF, 8), HALF)
    sums_ref[other] = e_fin[...]

    for step in range(1, N_RUN):
        w_copy(step).wait_send()
        b1_copy(step).wait_send()
        b2_copy(step).wait_send()
    for i in range(CHIPS - 1):
        e2_copy(i + 1).wait_send()
        for b in range(OWN):
            rs_copy(b * CHIPS + i).wait_send()
            ag_copy(i, b).wait_send()
    for i in range(CHIPS):
        for b in range(OWN):
            d_copy(b * CHIPS + i).wait_send()
            fw_copy(i, b).wait_send()
    e1.wait_send()
    e3.wait_send()
    f_copy.wait_send()


def last_kernel(nmt_ref, sums_ref, h_ref, nm_ref, nw_ref):
    nm_ref[...] = nmt_ref[...].T
    h = h_ref[...]
    matrix = sums_ref[:R] * mm(h.T, h)
    scaled, row, column, x, r = inverse_start(matrix)

    def more(carry):
        step, x, r = carry
        return (step < 10) & (jnp.max(jnp.abs(r)) > 1e-6)

    def body(carry):
        step, x, r = carry
        for _ in range(4):
            x, r = inverse_step(x, r)
        return step + 1, x, r

    _, x, r = lax.while_loop(more, body, (jnp.int32(0), x, r))
    x = inverse_polish(scaled, x)
    nw_ref[...] = mm(sums_ref[R:], x * row * column)[:RUN_DEV]


def per_device(spectra, mz_factor, mixing, run_weights, block_count, trim_scans):
    vmem = pl.BlockSpec(memory_space=pltpu.VMEM)
    smem = pl.BlockSpec(memory_space=pltpu.SMEM)
    dma8 = pltpu.SemaphoreType.DMA((8,))
    dma = pltpu.SemaphoreType.DMA
    half = (R + 16) // 2
    nmt, sums = pl.pallas_call(
        main_kernel,
        out_shape=(
            jax.ShapeDtypeStruct((R, WIDTH), F32),
            jax.ShapeDtypeStruct((R + 16, R), F32),
        ),
        in_specs=[pl.BlockSpec(memory_space=pl.ANY), vmem, vmem, vmem, smem, smem],
        out_specs=(vmem, vmem),
        scratch_shapes=[
            pltpu.VMEM((SLOTS * BLOCK, WIDTH), BF16),
            pltpu.VMEM((PIECES, CODED, R), jnp.int16),
            pltpu.VMEM((PIECES, CODED, R), jnp.int16),
            pltpu.VMEM((PIECES, BLOCK, R), F32),
            pltpu.VMEM((PIECES, CODED, R), jnp.int16),
            pltpu.VMEM((PIECES, CODED, R), jnp.int16),
            pltpu.VMEM((OWN, BLOCK, R), F32),
            pltpu.VMEM((2 * CHIPS, OWN, CODED, R), jnp.int16),
            pltpu.VMEM((SLOTS, 2 * R, BLOCK), BF16),
            pltpu.VMEM((SLOTS, R, R), F32),
            pltpu.VMEM((PAIR_RUNS, R, R), F32),
            pltpu.VMEM((PAIR_RUNS, R, R), F32),
            pltpu.VMEM((PAIR_RUNS, 2 * R, R), BF16),
            pltpu.VMEM((PAIR_RUNS, 2 * R, R), BF16),
            pltpu.VMEM((RUN_DEV, 2 * R, R), BF16),
            pltpu.VMEM((SLOTS, R, WIDTH), F32),
            pltpu.VMEM((RUN_DEV, R, WIDTH), F32),
            pltpu.VMEM((N_RUN, 16, R), F32),
            pltpu.VMEM((R, R), F32),
            pltpu.VMEM((R, R), F32),
            pltpu.VMEM((N_RUN, R // N_RUN, WIDTH), F32),
            pltpu.VMEM((N_RUN, R // N_RUN, WIDTH), F32),
            pltpu.VMEM((N_RUN, R // N_RUN, WIDTH), F32),
            pltpu.VMEM((R + 16, R), F32),
            pltpu.VMEM((R + 16, R), F32),
            pltpu.VMEM((half, R), F32),
            pltpu.VMEM((CHIPS, half, R), F32),
            pltpu.VMEM((half, R), F32),
            pltpu.VMEM((half, R), F32),
            dma((2 * CHIPS,)),
            dma((PIECES,)), dma((PIECES,)), dma((PIECES,)), dma((PIECES,)),
            dma((PIECES,)), dma((PIECES,)), dma((PIECES,)), dma((PIECES,)),
            dma8, dma8, dma8, dma8, dma8, dma8,
            dma, dma, dma8, dma8, dma, dma, dma, dma,
        ],
        compiler_params=pltpu.CompilerParams(
            collective_id=0, has_side_effects=True, vmem_limit_bytes=58 * 2**20
        ),
    )(spectra, mz_factor, mixing, run_weights, block_count, trim_scans)
    return pl.pallas_call(
        last_kernel,
        out_shape=(
            jax.ShapeDtypeStruct((WIDTH, R), F32),
            jax.ShapeDtypeStruct((RUN_DEV, R), F32),
        ),
        in_specs=[vmem, vmem, vmem],
        out_specs=(vmem, vmem),
    )(nmt, sums, mixing)


def solution(mesh):
    placed = (P("run", "mz"), P("mz", None), P(), P("run", None), P("run", None), P("run", None))
    return jax.shard_map(
        per_device,
        mesh=mesh,
        in_specs=placed,
        out_specs=(P("mz", None), P("run", None)),
        check_vma=False,
    )
```

time: 128 us -> 97.2 us (0.76)
  Pallas kernels: 128 us -> 96.4 us
    pallas_call x1, Pallas kernels: 123 us -> 92 us  [per_device(): pl.pallas_call(main_kernel, out_shape=(jax.ShapeDtypeStruct((R, WIDTH), F...]
where the time goes in v2:
time: 97.2 us; the launch traced here: 97.1 us
  Pallas kernels  96.4 us (99%)
    pallas_call x1, Pallas kernels, per_device(): pl.pallas_call(main_kernel, out_shape=(jax.ShapeDtypeStruct((R, WIDTH), F...  92 us
    pallas_call x1, Pallas kernels, per_device(): pl.pallas_call(last_kernel, out_shape=(jax.ShapeDtypeStruct((WIDTH, R), F...  4.48 us

profile of v2, /device:TPU:1, one launch (start us, length us, event | category | flops | bytes accessed | tf_op | source)
XLA Modules:
  0.0 97.1 jit_solution(7969569744465490378)
XLA Ops:
  0.6 92.0 %shard_map.77 = (f32[128,256]{1,0:T(8,128)}, f32[144,128]{1,0:T(8,128)}) custom-call(bf16[12288,256]{1,0:T(8,128)(2,1)} %x_hbm.1, bf16[256,128]{1,0:T(8,128)(2,1)} %v_ref.1, f32[128,128]{1,0:T(8,128)} %h_ref.3, f32[12,128]{1,0:T(8,128)} %w_ref.1, s32[1,12]{1,0:T(1,128)} %count_ref.1, s32[1,12]{1,0:T(1,128)} %trim_ref.1), custom_call_target="tpu_custom_call" | custom-call | tf_op jit(solution)/shard_map/pallas_call | solution.py:528
  92.6 4.5 %shard_map.78 = (f32[256,128]{1,0:T(8,128)}, f32[12,128]{1,0:T(8,128)}) custom-call(f32[128,256]{1,0:T(8,128)} %get-tuple-element.4.nmt_ref, f32[144,128]{1,0:T(8,128)} %get-tuple-element.5.sums_ref, f32[128,128]{1,0:T(8,128)} %h_ref.3), custom_call_target="tpu_custom_call" | custom-call | tf_op jit(solution)/shard_map/pallas_call | solution.py:576

commit v3 on v2

--- a/solution.py
+++ b/solution.py
@@ -214,29 +214,31 @@
     def rs_copy(t):
         return send(rs_send.at[t], rs_recv.at[t], rs_s.at[t], rs_r.at[t], peer(lax.rem(t, CHIPS) + 1))
 
-    def d_body(t, carry):
-        d_copy(t).start()
-        return carry
-
-    lax.fori_loop(0, PIECES, d_body, 0)
-
-    def reduce_body(b, carry):
-        first = b * CHIPS
+    def d_start(b):
         for i in range(CHIPS):
-            d_copy(first + i).wait_recv()
+            d_copy(b * CHIPS + i).start()
+
+    def rs_encode(b):
+        for i in range(CHIPS):
+            d_copy(b * CHIPS + i).wait_recv()
         for i in range(CHIPS - 1):
-            t = first + i
+            t = b * CHIPS + i
             encode(keep[t] + decode(drecv.at[t]), rs_send.at[t])
+        t = b * CHIPS + CHIPS - 1
+        acc[b] = keep[t] + decode(drecv.at[t])
+
+    def rs_start(b):
         for i in range(CHIPS - 1):
-            rs_copy(first + i).start()
-        t = first + CHIPS - 1
-        acc[b] = keep[t] + decode(drecv.at[t])
-        return carry
-
-    lax.fori_loop(0, OWN, reduce_body, 0)
-
+            rs_copy(b * CHIPS + i).start()
+
+    d_start(0)
     for step in range(1, N_RUN):
         w_copy(step).start()
+    rs_encode(0)
+    d_start(1)
+    rs_start(0)
+    d_start(2)
+    rs_encode(1)
 
     for step in range(1, N_RUN):
         w_copy(step, run_from(step)).wait_recv()
@@ -250,6 +252,15 @@
     def inv_body(i, carry):
         return inverse_step(*carry)
 
+    x0, r0 = lax.fori_loop(0, INV_STEPS[0], inv_body, (x0, r0))
+    rs_start(1)
+    rs_encode(2)
+    x0, r0 = lax.fori_loop(0, INV_STEPS[1], inv_body, (x0, r0))
+    rs_start(2)
+    x0, r0 = lax.fori_loop(0, INV_STEPS[2], inv_body, (x0, r0))
+    x0 = inverse_polish(scaled, x0)
+    x0 = inverse_polish(scaled, x0)
+    cinv[...] = x0 * row * column
     own_weights = jnp.concatenate([weights, jnp.zeros((R - 16, R), F32)], axis=0)
     wt[...] = own_weights.T
 
@@ -297,11 +308,6 @@
             gram[block] = (out[:R, :R] + out[R:, R:]) + (out[:R, R:] + out[R:, :R])
 
     for b in range(OWN):
-        x0, r0 = lax.fori_loop(0, INV_STEPS[b], inv_body, (x0, r0))
-        if b == OWN - 1:
-            x0 = inverse_polish(scaled, x0)
-            x0 = inverse_polish(scaled, x0)
-            cinv[...] = x0 * row * column
         own = acc[b]
         for i in range(CHIPS - 1):
             rs_copy(b * CHIPS + i).wait_recv()
@@ -316,10 +322,11 @@
         for i in range(CHIPS - 1):
             ag_copy(i, b).start()
         fw_copy(CHIPS - 1, b).start()
-
+        if b:
+            take_pair(CHIPS - 1, b - 1)
+
+    take_pair(CHIPS - 1, OWN - 1)
     late = []
-    for b in range(OWN):
-        take_pair(CHIPS - 1, b)
     for b in range(OWN):
         for i in range(CHIPS - 1):
             ag_copy(i, b, source(i) * 2 + core).wait_recv()

time: 97.2 us -> 90.3 us (0.929)
  Pallas kernels: 96.4 us -> 89.5 us
    pallas_call x1, Pallas kernels: 92 us -> 85.1 us  [per_device(): pl.pallas_call(main_kernel, out_shape=(jax.ShapeDtypeStruct((R, WIDTH), F...]
where the time goes in v3:
time: 90.3 us; the launch traced here: 90.2 us
  Pallas kernels  89.5 us (99%)
    pallas_call x1, Pallas kernels, per_device(): pl.pallas_call(main_kernel, out_shape=(jax.ShapeDtypeStruct((R, WIDTH), F...  85.1 us
    pallas_call x1, Pallas kernels, per_device(): pl.pallas_call(last_kernel, out_shape=(jax.ShapeDtypeStruct((WIDTH, R), F...  4.48 us

profile of v3, /device:TPU:1, one launch (start us, length us, event | category | flops | bytes accessed | tf_op | source)
XLA Modules:
  0.0 90.2 jit_solution(8542002304205358075)
XLA Ops:
  0.6 85.1 %shard_map.77 = (f32[128,256]{1,0:T(8,128)}, f32[144,128]{1,0:T(8,128)}) custom-call(bf16[12288,256]{1,0:T(8,128)(2,1)} %x_hbm.1, bf16[256,128]{1,0:T(8,128)(2,1)} %v_ref.1, f32[128,128]{1,0:T(8,128)} %h_ref.3, f32[12,128]{1,0:T(8,128)} %w_ref.1, s32[1,12]{1,0:T(1,128)} %count_ref.1, s32[1,12]{1,0:T(1,128)} %trim_ref.1), custom_call_target="tpu_custom_call" | custom-call | tf_op jit(solution)/shard_map/pallas_call | solution.py:535
  85.7 4.5 %shard_map.78 = (f32[256,128]{1,0:T(8,128)}, f32[12,128]{1,0:T(8,128)}) custom-call(f32[128,256]{1,0:T(8,128)} %get-tuple-element.4.nmt_ref, f32[144,128]{1,0:T(8,128)} %get-tuple-element.5.sums_ref, f32[128,128]{1,0:T(8,128)} %h_ref.3), custom_call_target="tpu_custom_call" | custom-call | tf_op jit(solution)/shard_map/pallas_call | solution.py:583

commit v4 on v3

--- a/solution.py
+++ b/solution.py
@@ -27,6 +27,8 @@
 
 OFFSETS = ((1, 0), (3, 0), (0, 1), (2, 0), (1, 1), (3, 1), (2, 1))
 
+FAR_FIRST = (4, 5, 3, 6, 2, 7, 1)
+
 MESH = pl.DeviceIdType.MESH
 F32 = jnp.float32
 BF16 = jnp.bfloat16
@@ -135,9 +137,9 @@
     x_hbm, v_ref, h_ref, w_ref, count_ref, trim_ref,
     nmt_ref, sums_ref,
     xv, dsend, drecv, keep, rs_send, rs_recv, acc, agbuf, st, gram, gs, qs, f_own, f_sib, ft, zb, us,
-    wall, cinv, wt, bpart, brecv, ball, e_part, e_sib, e_half, e_recv, e_out, e_fin,
+    wall, mix, cinv, wt, bpart, brecv, ball, e_gram, e_gram_sib, e_all, e_part, e_sib, e_half, e_recv, e_out, e_fin,
     xsem, d_s, d_r, rs_s, rs_r, ag_s, ag_r, fw_s, fw_r, w_s, w_r, b1_s, b1_r, b2_s, b2_r,
-    e1_s, e1_r, e2_s, e2_r, e3_s, e3_r, f_s, f_r,
+    e1_s, e1_r, e2_s, e2_r, e3_s, e3_r, f_s, f_r, eg_s, eg_r,
 ):
     run = lax.axis_index("run")
     me = lax.axis_index("mz")
@@ -154,6 +156,12 @@
     def run_peer(step):
         return (lax.rem(run + step, N_RUN), me)
 
+    barrier = pltpu.get_barrier_semaphore()
+    pl.semaphore_signal(barrier, inc=1, device_id=sibling, device_id_type=MESH)
+    for step in FAR_FIRST:
+        pl.semaphore_signal(barrier, inc=1, device_id=peer(step), device_id_type=MESH)
+        pl.semaphore_signal(barrier, inc=1, device_id=run_peer(step), device_id_type=MESH)
+
     def x_chunk(step, side):
         return chip_at(step + 1) * 2 + (core if side else 1 - core)
 
@@ -164,12 +172,6 @@
     for step in range(CHIPS):
         x_copy(step, 0).start()
         x_copy(step, 1).start()
-
-    barrier = pltpu.get_barrier_semaphore()
-    pl.semaphore_signal(barrier, inc=1, device_id=sibling, device_id_type=MESH)
-    for step in range(1, CHIPS):
-        pl.semaphore_signal(barrier, inc=1, device_id=peer(step), device_id_type=MESH)
-        pl.semaphore_signal(barrier, inc=1, device_id=run_peer(step), device_id_type=MESH)
 
     weights = jnp.concatenate([w_ref[...], jnp.zeros((16 - RUN_DEV, R), F32)], axis=0)
     wall[run] = weights
@@ -245,8 +247,8 @@
     all_weights = wall[...].reshape(N_RUN * 16, R)
     h = h_ref[...]
     ht = h.T
-    mix_gram = mm(ht, h)
-    c_matrix = mm(all_weights.T, all_weights) * mix_gram
+    mix[...] = mm(ht, h)
+    c_matrix = mm(all_weights.T, all_weights) * mix[...]
     scaled, row, column, x0, r0 = inverse_start(c_matrix)
 
     def inv_body(i, carry):
@@ -373,7 +375,8 @@
             qs[j] = products[j]
         return carry
 
-    lax.fori_loop(0, NSTEPS - 1, newton_body, 0)
+    for i in range(NSTEPS - 1):
+        newton_body(i, 0)
 
     lasts = [mm(qs[j], 1.5 * unit - 0.5 * gs[j]) for j in pair_runs]
     lasts = [mm(lasts[j], h * w_ref[pl.ds(first_run + j, 1), :]) for j in pair_runs]
@@ -441,14 +444,14 @@
     def b2_copy(step, slot=run):
         return send(ball.at[slot], ball.at[slot], b2_s.at[step], b2_r.at[step], run_peer(step))
 
-    for step in range(1, N_RUN):
+    for step in FAR_FIRST:
         b1_copy(step).start()
     own = bpart[run]
     for step in range(1, N_RUN):
         b1_copy(step).wait_recv()
         own = own + brecv[step]
     ball[run] = own
-    for step in range(1, N_RUN):
+    for step in FAR_FIRST:
         b2_copy(step).start()
     for step in range(1, N_RUN):
         b2_copy(step, run_from(step)).wait_recv()
@@ -456,25 +459,30 @@
     nmt = wide(stack_left(cinv[...]), ball[...].reshape(R, WIDTH))
     nmt_ref[...] = nmt
 
-    e_part[:R] = self_gram(nmt)
+    e_gram[...] = self_gram(nmt)
+    e1g = send(e_gram, e_gram_sib, eg_s, eg_r, sibling)
+    e1g.start()
     columns = jnp.zeros((R, R), F32)
     lanes = lax.broadcasted_iota(jnp.int32, (R, R), 1)
     for k in range(RUN_DEV):
         col = jnp.sum(us[k] * nmt, axis=1, keepdims=True)
         columns = jnp.where(lanes == k, col, columns)
-    e_part[R:] = columns.T[:16]
+    e_part[...] = columns.T[:16]
 
     HALF = (R + 16) // 2
     e1 = send(e_part, e_sib, e1_s, e1_r, sibling)
     e1.start()
+    e1g.wait_recv()
     e1.wait_recv()
+    e_all[:R] = e_gram[...] + e_gram_sib[...]
+    e_all[R:] = e_part[...] + e_sib[...]
     mine = pl.ds(pl.multiple_of(core * HALF, 8), HALF)
-    e_half[...] = e_part[mine] + e_sib[mine]
+    e_half[...] = e_all[mine]
 
     def e2_copy(step, slot=chip):
         return send(e_half, e_recv.at[slot], e2_s.at[step], e2_r.at[step], peer(step))
 
-    for step in range(1, CHIPS):
+    for step in FAR_FIRST:
         e2_copy(step).start()
     e_recv[chip] = e_half[...]
     for step in range(1, CHIPS):
@@ -486,6 +494,7 @@
     e3.wait_recv()
     other = pl.ds(pl.multiple_of((1 - core) * HALF, 8), HALF)
     sums_ref[other] = e_fin[...]
+    sums_ref[:R] = sums_ref[:R] * mix[...]
 
     for step in range(1, N_RUN):
         w_copy(step).wait_send()
@@ -501,15 +510,14 @@
             d_copy(b * CHIPS + i).wait_send()
             fw_copy(i, b).wait_send()
     e1.wait_send()
+    e1g.wait_send()
     e3.wait_send()
     f_copy.wait_send()
 
 
-def last_kernel(nmt_ref, sums_ref, h_ref, nm_ref, nw_ref):
+def last_kernel(nmt_ref, sums_ref, nm_ref, nw_ref):
     nm_ref[...] = nmt_ref[...].T
-    h = h_ref[...]
-    matrix = sums_ref[:R] * mm(h.T, h)
-    scaled, row, column, x, r = inverse_start(matrix)
+    scaled, row, column, x, r = inverse_start(sums_ref[:R])
 
     def more(carry):
         step, x, r = carry
@@ -561,11 +569,15 @@
             pltpu.VMEM((N_RUN, 16, R), F32),
             pltpu.VMEM((R, R), F32),
             pltpu.VMEM((R, R), F32),
+            pltpu.VMEM((R, R), F32),
             pltpu.VMEM((N_RUN, R // N_RUN, WIDTH), F32),
             pltpu.VMEM((N_RUN, R // N_RUN, WIDTH), F32),
             pltpu.VMEM((N_RUN, R // N_RUN, WIDTH), F32),
+            pltpu.VMEM((R, R), F32),
+            pltpu.VMEM((R, R), F32),
             pltpu.VMEM((R + 16, R), F32),
-            pltpu.VMEM((R + 16, R), F32),
+            pltpu.VMEM((16, R), F32),
+            pltpu.VMEM((16, R), F32),
             pltpu.VMEM((half, R), F32),
             pltpu.VMEM((CHIPS, half, R), F32),
             pltpu.VMEM((half, R), F32),
@@ -574,7 +586,7 @@
             dma((PIECES,)), dma((PIECES,)), dma((PIECES,)), dma((PIECES,)),
             dma((PIECES,)), dma((PIECES,)), dma((PIECES,)), dma((PIECES,)),
             dma8, dma8, dma8, dma8, dma8, dma8,
-            dma, dma, dma8, dma8, dma, dma, dma, dma,
+            dma, dma, dma8, dma8, dma, dma, dma, dma, dma, dma,
         ],
         compiler_params=pltpu.CompilerParams(
             collective_id=0, has_side_effects=True, vmem_limit_bytes=58 * 2**20
@@ -586,9 +598,9 @@
             jax.ShapeDtypeStruct((WIDTH, R), F32),
             jax.ShapeDtypeStruct((RUN_DEV, R), F32),
         ),
-        in_specs=[vmem, vmem, vmem],
+        in_specs=[vmem, vmem],
         out_specs=(vmem, vmem),
-    )(nmt, sums, mixing)
+    )(nmt, sums)
 
 
 def solution(mesh):

time: 90.3 us -> 88.8 us (0.983)
  Pallas kernels: 89.5 us -> 88 us
    pallas_call x1, Pallas kernels: 85.1 us -> 83.7 us  [per_device(): pl.pallas_call(main_kernel, out_shape=(jax.ShapeDtypeStruct((R, WIDTH), F...]
where the time goes in v4:
time: 88.8 us; the launch traced here: 88.6 us
  Pallas kernels  88 us (99%)
    pallas_call x1, Pallas kernels, per_device(): pl.pallas_call(main_kernel, out_shape=(jax.ShapeDtypeStruct((R, WIDTH), F...  83.7 us
    pallas_call x1, Pallas kernels, per_device(): pl.pallas_call(last_kernel, out_shape=(jax.ShapeDtypeStruct((WIDTH, R), F...  4.28 us

profile of v4, /device:TPU:1, one launch (start us, length us, event | category | flops | bytes accessed | tf_op | source)
XLA Modules:
  0.0 88.6 jit_solution(10469703737321322578)
XLA Ops:
  0.6 83.7 %shard_map.77 = (f32[128,256]{1,0:T(8,128)}, f32[144,128]{1,0:T(8,128)}) custom-call(bf16[12288,256]{1,0:T(8,128)(2,1)} %x_hbm.1, bf16[256,128]{1,0:T(8,128)(2,1)} %v_ref.1, f32[128,128]{1,0:T(8,128)} %h_ref.1, f32[12,128]{1,0:T(8,128)} %w_ref.1, s32[1,12]{1,0:T(1,128)} %count_ref.1, s32[1,12]{1,0:T(1,128)} %trim_ref.1), custom_call_target="tpu_custom_call" | custom-call | tf_op jit(solution)/shard_map/pallas_call | solution.py:543
  84.3 4.3 %shard_map.78 = (f32[256,128]{1,0:T(8,128)}, f32[12,128]{1,0:T(8,128)}) custom-call(f32[128,256]{1,0:T(8,128)} %get-tuple-element.4.nmt_ref, f32[144,128]{1,0:T(8,128)} %get-tuple-element.5.sums_ref), custom_call_target="tpu_custom_call" | custom-call | tf_op jit(solution)/shard_map/pallas_call | solution.py:595

commit v5 on v4

--- a/solution.py
+++ b/solution.py
@@ -236,9 +236,16 @@
     d_start(0)
     for step in range(1, N_RUN):
         w_copy(step).start()
-    rs_encode(0)
+    for part in (range(3), range(3, CHIPS - 1)):
+        for i in part:
+            d_copy(i).wait_recv()
+        for i in part:
+            encode(keep[i] + decode(drecv.at[i]), rs_send.at[i])
+        for i in part:
+            rs_copy(i).start()
+    d_copy(CHIPS - 1).wait_recv()
+    acc[0] = keep[CHIPS - 1] + decode(drecv.at[CHIPS - 1])
     d_start(1)
-    rs_start(0)
     d_start(2)
     rs_encode(1)
 

time: 88.8 us -> 88.2 us (level)
  no operation moved by 1% of the time
where the time goes in v5:
time: 88.2 us; the launch traced here: 87.9 us
  Pallas kernels  87.2 us (99%)
    pallas_call x1, Pallas kernels, per_device(): pl.pallas_call(main_kernel, out_shape=(jax.ShapeDtypeStruct((R, WIDTH), F...  82.9 us
    pallas_call x1, Pallas kernels, per_device(): pl.pallas_call(last_kernel, out_shape=(jax.ShapeDtypeStruct((WIDTH, R), F...  4.28 us

profile of v5, /device:TPU:1, one launch (start us, length us, event | category | flops | bytes accessed | tf_op | source)
XLA Modules:
  0.0 87.9 jit_solution(11219692890471066498)
XLA Ops:
  0.6 82.9 %shard_map.77 = (f32[128,256]{1,0:T(8,128)}, f32[144,128]{1,0:T(8,128)}) custom-call(bf16[12288,256]{1,0:T(8,128)(2,1)} %x_hbm.1, bf16[256,128]{1,0:T(8,128)(2,1)} %v_ref.1, f32[128,128]{1,0:T(8,128)} %h_ref.1, f32[12,128]{1,0:T(8,128)} %w_ref.1, s32[1,12]{1,0:T(1,128)} %count_ref.1, s32[1,12]{1,0:T(1,128)} %trim_ref.1), custom_call_target="tpu_custom_call" | custom-call | tf_op jit(solution)/shard_map/pallas_call | solution.py:550
  83.6 4.3 %shard_map.78 = (f32[256,128]{1,0:T(8,128)}, f32[12,128]{1,0:T(8,128)}) custom-call(f32[128,256]{1,0:T(8,128)} %get-tuple-element.4.nmt_ref, f32[144,128]{1,0:T(8,128)} %get-tuple-element.5.sums_ref), custom_call_target="tpu_custom_call" | custom-call | tf_op jit(solution)/shard_map/pallas_call | solution.py:602

commit v6 on v5

--- a/solution.py
+++ b/solution.py
@@ -402,8 +402,8 @@
 
     def project(group):
         polars = []
-        for u in range(8):
-            block = group * 8 + u
+        for u in range(12):
+            block = group * 12 + u
             owner = jnp.int32(0)
             end = jnp.int32(0)
             for k in range(RUN_DEV - 1):
@@ -414,12 +414,12 @@
                 jnp.concatenate([factor, factor], axis=1), st[block], preferred_element_type=F32
             )
             polars.append((out[:R] + out[R:]).astype(BF16))
-        for u in range(8):
-            block = group * 8 + u
+        for u in range(12):
+            block = group * 12 + u
             rows = slice(block * BLOCK, (block + 1) * BLOCK)
             zb[block] = jnp.dot(polars[u], xv[rows, :], preferred_element_type=F32)
 
-    for group in range(SLOTS // 8):
+    for group in range(SLOTS // 12):
         project(group)
 
     left_h = stack_left(h.T)

time: 88.2 us -> 88.3 us (level)
  no operation moved by 1% of the time
where the time goes in v6:
time: 88.3 us; the launch traced here: 87.9 us
  Pallas kernels  87.3 us (99%)
    pallas_call x1, Pallas kernels, per_device(): pl.pallas_call(main_kernel, out_shape=(jax.ShapeDtypeStruct((R, WIDTH), F...  83 us
    pallas_call x1, Pallas kernels, per_device(): pl.pallas_call(last_kernel, out_shape=(jax.ShapeDtypeStruct((WIDTH, R), F...  4.28 us

profile of v6, /device:TPU:1, one launch (start us, length us, event | category | flops | bytes accessed | tf_op | source)
XLA Modules:
  0.0 87.9 jit_solution(11705936028918427970)
XLA Ops:
  0.6 83.0 %shard_map.77 = (f32[128,256]{1,0:T(8,128)}, f32[144,128]{1,0:T(8,128)}) custom-call(bf16[12288,256]{1,0:T(8,128)(2,1)} %x_hbm.1, bf16[256,128]{1,0:T(8,128)(2,1)} %v_ref.1, f32[128,128]{1,0:T(8,128)} %h_ref.1, f32[12,128]{1,0:T(8,128)} %w_ref.1, s32[1,12]{1,0:T(1,128)} %count_ref.1, s32[1,12]{1,0:T(1,128)} %trim_ref.1), custom_call_target="tpu_custom_call" | custom-call | tf_op jit(solution)/shard_map/pallas_call | solution.py:550
  83.7 4.3 %shard_map.78 = (f32[256,128]{1,0:T(8,128)}, f32[12,128]{1,0:T(8,128)}) custom-call(f32[128,256]{1,0:T(8,128)} %get-tuple-element.4.nmt_ref, f32[144,128]{1,0:T(8,128)} %get-tuple-element.5.sums_ref), custom_call_target="tpu_custom_call" | custom-call | tf_op jit(solution)/shard_map/pallas_call | solution.py:602
